TPU v7x, 128 devices: a whole 4x4x4 slice. The times are simulated.
128 devices in a mesh: var: 8 (over y, z_hi), row: 16 (over z_lo, x, core).
Axes of the slice: x: 4, y: 4, z: 4 (z_hi: 2, z_lo: 2; z = z_hi * 2 + z_lo), core: 2. Of those that a mesh axis runs over, the one named last changes fastest.
Arguments:
- frf: float32 [2, 65536, 1024], P(None, 'row', 'var'), may hold values from -0.078125 to 0.078125
- mount_rows: int32 [256, 4], replicated, may hold values from 0 to 65535, as said below
- recv_rows: int32 [512], replicated, may hold values from 0 to 65535
- codes: int32 [32768, 256], P(('var', 'row')), may hold values from 0 to 7
- stiffness: float32 [8, 4], replicated, may hold values from 0.3 to 0.9
- loss: float32 [8, 4], replicated, may hold values from 0.05 to 0.4
- load: float32 [2, 1024], replicated, may hold values from -6 to 6
Outputs:
- response: float32 [2, 32768, 512], P(None, ('var', 'row'))
Inputs may be any that keep to these rules, and one draw needn't show every extreme that they name: `mount_rows`: the 1024 rows are distinct and increasing; entry k of the flattened table lies in [k * (65536 / 1024), (k + 1) * (65536 / 1024)).
All inputs are finite; a program needn't handle non-finite values.
Results may differ from a plain program's by a relative error of at most 0.0001.
Values sent between devices are 32-bit elements; how exact they have to be, the bound alone decides.
A program may use at most 128 MiB of HBM per device.

v0:
```python
import functools

import jax
import jax.numpy as jnp
from jax import lax
from jax.experimental import pallas as pl
from jax.experimental.pallas import tpu as pltpu
from jax.sharding import PartitionSpec as P

MESH = pl.DeviceIdType.MESH
F32, BF16 = jnp.float32, jnp.bfloat16
ITERS = 4
LEVELS = 8
GRANULE = ((0, 0), (0, 1), (0, 2), (1, 0), (1, 1), (1, 2), (2, 0), (2, 1))
PART = (3, 3, 2)
ORDER = (1, 3, 2)
NREC = 20


def device(x, y, z, k):
    return {"var": y * 2 + z // 2, "row": (z % 2) * 8 + x * 2 + k}


class Net:
    def __init__(self):
        v, r = lax.axis_index("var"), lax.axis_index("row")
        y, zh = v // 2, v % 2
        zl, x, k = r // 8, (r // 2) % 4, r % 2
        z = zh * 2 + zl
        self.v, self.r, self.zl, self.zh, self.k = v, r, zl, zh, k
        self.pos = (x, y, z)
        self.near = {}
        for a in range(3):
            for d in (1, 2, 3):
                c = [x, y, z]
                c[a] = (c[a] + d) % 4
                self.near[a, d] = device(*c, k)
        self.sib = device(x, y, z, 1 - k)
        self.pair = {"var": v, "row": (1 - zl) * 8 + x * 2 + k}
        self.same_row = [{"var": (v + i) % 8, "row": r} for i in range(1, 8)]
        self.same_var = [{"var": v, "row": (r + i) % 16} for i in range(1, 16)]

    def along(self, turn, d):
        m, n = self.near[turn % 3, d], self.near[(turn + 1) % 3, d]
        return {q: jnp.where(self.k == 0, m[q], n[q]) for q in ("var", "row")}

    def greet(self):
        sem = pltpu.get_barrier_semaphore()
        for d in list(self.near.values()) + self.same_row + self.same_var:
            pl.semaphore_signal(sem, inc=1, device_id=d, device_id_type=MESH)

    def greeted(self):
        pl.semaphore_wait(pltpu.get_barrier_semaphore(), 9 + 7 + 15)


def slot(k, d3, d2, d1=0, n=1):
    return pl.ds(((k * 4 + d3) * 4 + d2) * 4 + d1, n)


class Gather:
    def __init__(self, group, bufs, send, recv, net, size_ref):
        self.group, self.bufs, self.net, self.size_ref = group, bufs, net, size_ref
        self.send, self.recv = send.at[group], recv
        self.count = 0

    def sem(self, kind, i=0):
        return self.recv.at[self.group * NREC + {"a": 0, "b": 0, "c": 4, "s": 16}[kind] + i]

    def go(self, p, src, dst, sem, dev):
        pltpu.make_async_remote_copy(
            src_ref=self.bufs[p].at[src], dst_ref=self.bufs[p].at[dst], send_sem=self.send, recv_sem=sem,
            device_id=dev, device_id_type=MESH).start()

    def wait(self, n, sem):
        ref = self.size_ref.at[pl.ds(0, n)]
        pltpu.make_async_copy(ref, ref, sem).wait()

    def dev(self, p, axis, d):
        return self.net.along(p + axis - 1 + self.group, d)

    def first(self):
        k = self.net.k
        for p in range(3):
            for d in ORDER:
                self.go(p, slot(k, 0, 0), slot(k, 0, 0, 4 - d), self.sem("a"), self.dev(p, 1, d))
        for p in range(3):
            self.send_b(p, (0, 1))
        for p in range(3):
            self.send_c(p, 0, (0, 1))

    def send_b(self, p, what):
        k = self.net.k
        for d in ORDER:
            self.go(p, slot(k, 0, 0, *what), slot(k, 0, 4 - d, *what), self.sem("b", d), self.dev(p, 2, d))

    def send_c(self, p, d2, what):
        k = self.net.k
        for d in ORDER:
            self.go(p, slot(k, 0, d2, *what), slot(k, 4 - d, d2, *what), self.sem("c", d2 * 3 + d - 1), self.dev(p, 3, d))

    def core(self, d3, d2):
        at = slot(self.net.k, d3, d2, 0, 4)
        for p in range(3):
            self.go(p, at, at, self.sem("s", d3), self.net.sib)

    def second(self):
        self.wait(3, self.sem("a"))
        for p in range(3):
            self.send_b(p, (1, 3))
        for p in range(3):
            self.send_c(p, 0, (1, 3))
        self.core(0, 0)

    def third(self, d):
        self.wait(4, self.sem("b", d))
        for p in range(3):
            self.send_c(p, 4 - d, (0, 4))
        self.core(0, 4 - d)

    def last(self, d2, d):
        self.wait(4, self.sem("c", d2 * 3 + d - 1))
        self.core(4 - d, d2)

    def lasts(self, *lines):
        for d2 in lines:
            for d in ORDER:
                self.last(d2, d)

    def cores(self):
        for d3 in range(4):
            self.wait(16, self.sem("s", d3))

    def end(self, frf_v):
        ref = frf_v.at[:, pl.ds(0, 127 * 32), :]
        pltpu.make_async_copy(ref, ref, self.send).wait()


def halves(x):
    hi = x.astype(BF16)
    return hi, (x - hi.astype(F32)).astype(BF16)


def put(ref, base, rows, cols, re, im):
    for i, x in enumerate((re, im, re + im)):
        hi, lo = halves(x)
        ref[base + 2 * i, rows, cols] = hi
        ref[base + 2 * i + 1, rows, cols] = lo


def split(net, gather, mats, row_base):
    for k in range(2):
        axes = [[(p + q + k + gather.group) % 3 for q in range(3)] for p in range(3)]

        def body(i, _, k=k, axes=axes):
            far = (i % 4, (i // 4) % 4, i // 16)
            at = [(net.pos[a] + far[a]) % 4 for a in range(3)]
            row = (at[2] % 2) * 8 + at[0] * 2 + k
            col = at[1] * 2 + at[2] // 2
            src = [((k * 4 + far[a3]) * 4 + far[a2]) * 4 + far[a1] for a1, a2, a3 in axes]
            cols = pl.ds(pl.multiple_of(col * 128, 128), 128)
            tile = [gather.bufs[p][src[p], g] for p, g in GRANULE]
            for t in range(2):
                re = jnp.concatenate([tile[2 * t], tile[2 * t + 1]], 0)
                im = jnp.concatenate([tile[4 + 2 * t], tile[5 + 2 * t]], 0)
                rows = pl.ds(pl.multiple_of(row_base + row * 32 + t * 16, 16), 16)
                put(mats, 0, rows, cols, re, im)
            return 0

        lax.fori_loop(0, 64, body, 0, unroll=2)


def product(mats, rows, z, base):
    dot = functools.partial(jnp.dot, preferred_element_type=F32)
    out = []
    for i in range(3):
        a_hi, a_lo = mats[2 * i, rows, :], mats[2 * i + 1, rows, :]
        z_hi, z_lo = z[base + 2 * i], z[base + 2 * i + 1]
        out.append(dot(a_hi, z_hi) + (dot(a_hi, z_lo) + dot(a_lo, z_hi)))
    return out[0] - out[1], out[2] - out[0] - out[1]


def wide(x):
    return jnp.concatenate([x, x], 1)


def kernel(frf, mount, recv_rows, codes, stiffness, loss, load, out, frf_v, *refs):
    h0, h1, rb = refs[0:3], refs[3:6], refs[6:9]
    amat, rmat, z, delta, load_c, y1_c, picked, sum1, got1, got2, got3, y1_own, y1_part, y1_sum, y1_all = refs[9:24]
    send, recv, misc_send, misc_recv, local = refs[24:]
    net = Net()
    k = net.k
    whole = pltpu.make_async_copy(frf, frf_v, local)
    whole.start()
    net.greet()
    lane = lax.broadcasted_iota(jnp.int32, (8, 128), 1)
    sub = lax.broadcasted_iota(jnp.int32, (8, 128), 0)

    def column(tile, at):
        return jnp.broadcast_to(jnp.sum(jnp.where(lane == sub + at, tile, 0.0), axis=1, keepdims=True), (8, 128))

    gathers = [Gather(i, bufs, send, recv, net, picked) for i, bufs in enumerate((h0, h1, rb))]
    whole.wait()

    first_row = net.r * 4096
    cols = pl.ds(pl.multiple_of(net.v * 128, 128), 128)
    l_re = jnp.broadcast_to(load[0:1, cols], (8, 128))
    l_im = jnp.broadcast_to(load[1:2, cols], (8, 128))
    part = jnp.zeros((8, 128), F32)
    for t in range(8):
        at = [jnp.clip(mount[net.r * 64 + t * 8 + s] - first_row, 0, 4095) for s in range(8)]
        re, im = (jnp.concatenate([frf_v[c, pl.ds(i, 1), :] for i in at], 0) for c in range(2))
        for c, x in ((0, re), (1, im)):
            p, g = GRANULE[c * 4 + t % 4]
            (h0, h1)[t // 4][p][k * 64, g] = x
        y_re = jnp.sum(re * l_re - im * l_im, axis=1, keepdims=True)
        y_im = jnp.sum(re * l_im + im * l_re, axis=1, keepdims=True)
        part = part + jnp.where(lane == sub + t * 8, y_re, 0.0) + jnp.where(lane == sub + 64 + t * 8, y_im, 0.0)
    y1_own[0] = part
    net.greeted()

    def spread(src, dst, i, devs):
        for n, dev in enumerate(devs):
            pltpu.make_async_remote_copy(
                src_ref=src.at[0], dst_ref=dst.at[n], send_sem=misc_send.at[i], recv_sem=misc_recv.at[i],
                device_id=dev, device_id_type=MESH).start()

    def settle(ref, i):
        pltpu.make_async_copy(ref, ref, misc_send.at[i]).wait()

    def arrive(ref, i):
        pltpu.make_async_copy(ref, ref, misc_recv.at[i]).wait()

    spread(y1_own, y1_part, 0, net.same_row)
    gathers[0].first()
    gathers[1].first()

    def pick(b, _):
        zl, x, kk = b // 8, (b // 2) % 4, b % 2
        to = (kk * 4 + x) * 2 + zl
        for t in range(4):
            at = [recv_rows[b * 32 + t * 8 + s] - first_row for s in range(8)]
            inside = [(i >= 0) & (i < 4096) for i in at]
            at = [jnp.clip(i, 0, 4095) for i in at]
            for c in range(2):
                x8 = [jnp.where(inside[s], frf_v[c, pl.ds(at[s], 1), :], 0.0) for s in range(8)]
                picked[to, c * 4 + t] = jnp.concatenate(x8, 0)
        return 0

    lax.fori_loop(0, 16, pick, 0)
    mine, other = pl.ds(k * 8, 8), pl.ds((1 - k) * 8, 8)
    pltpu.make_async_remote_copy(
        src_ref=picked.at[other], dst_ref=got1, send_sem=misc_send.at[2], recv_sem=misc_recv.at[2],
        device_id=net.sib, device_id_type=MESH).start()

    gathers[0].second()
    gathers[1].second()

    arrive(y1_part, 0)
    total = y1_own[0]
    for i in range(7):
        total = total + y1_part[i]
    y1_sum[0] = total
    spread(y1_sum, y1_all, 1, net.same_var)

    arrive(got1, 2)
    sum1[...] = picked[mine] + got1[...]
    xx = net.pos[0]
    for n, d in enumerate((1, 2, 3)):
        pltpu.make_async_remote_copy(
            src_ref=sum1.at[pl.ds(((xx + d) % 4) * 2, 2)], dst_ref=got2.at[pl.ds(n * 2, 2)],
            send_sem=misc_send.at[3], recv_sem=misc_recv.at[3], device_id=net.near[0, d], device_id_type=MESH).start()

    for d in ORDER:
        gathers[0].third(d)
    for d in ORDER:
        gathers[1].third(d)

    arrive(got2, 3)
    sums = [sum1[xx * 2 + i] + got2[i] + got2[2 + i] + got2[4 + i] for i in range(2)]
    for i in range(2):
        got1[i] = sums[i]
    pltpu.make_async_remote_copy(
        src_ref=got1.at[1 - net.zl], dst_ref=got3, send_sem=misc_send.at[4], recv_sem=misc_recv.at[4],
        device_id=net.pair, device_id_type=MESH).start()

    def load_columns(j, _):
        rows = pl.ds(pl.multiple_of(j * 8, 8), 8)
        c128 = pl.ds(pl.multiple_of((j // 16) * 128, 128), 128)
        for c in range(2):
            load_c[c, rows, :] = column(jnp.broadcast_to(load[c : c + 1, c128], (8, 128)), (j % 16) * 8)
        return 0

    lax.fori_loop(0, 128, load_columns, 0)

    def table(ref):
        quarter = lax.broadcasted_iota(jnp.int32, (8, 256), 0) % 4
        out = []
        for l in range(LEVELS):
            x = jnp.where(quarter == 0, ref[l, 0], ref[l, 1])
            out.append(jnp.where(quarter == 2, ref[l, 2], jnp.where(quarter == 3, ref[l, 3], x)))
        return out

    code_b = codes[...].astype(F32).astype(BF16)
    for b in range(4):
        mount_of = lax.broadcasted_iota(jnp.int32, (256, 256), 0) // 4 + b * 64
        rep = (mount_of == lax.broadcasted_iota(jnp.int32, (256, 256), 1)).astype(F32).astype(BF16)
        delta[0, pl.ds(b * 256, 256), :] = lax.dot_general(rep, code_b, (((1,), (1,)), ((), ())), preferred_element_type=F32)
    stiff_t, loss_t = table(stiffness), table(loss)

    def look(j, _):
        rows = pl.ds(pl.multiple_of(j * 8, 8), 8)
        code = delta[0, rows, :]
        s, e = stiff_t[0], loss_t[0]
        for l in range(1, LEVELS):
            here = code == float(l)
            s, e = jnp.where(here, stiff_t[l], s), jnp.where(here, loss_t[l], e)
        delta[0, rows, :] = s
        delta[1, rows, :] = s * e
        return 0

    lax.fori_loop(0, 128, look, 0)

    arrive(y1_all, 1)
    y1_c[pl.ds(net.r * 8, 8), :] = y1_sum[0]
    for i in range(15):
        y1_c[pl.ds(((net.r + 15 - i) % 16) * 8, 8), :] = y1_all[i]

    def step(rows, y_re, y_im, to):
        d_re, d_im = delta[0, rows, :], delta[1, rows, :]
        z_re = wide(load_c[0, rows, :]) - (d_re * y_re - d_im * y_im)
        z_im = wide(load_c[1, rows, :]) - (d_re * y_im + d_im * y_re)
        put(z, to, rows, slice(None), z_re, z_im)

    def begin(j, _):
        tile = y1_c[pl.ds(pl.multiple_of((j // 4) * 8, 8), 8), :]
        at = (j % 4) * 16
        y_re, y_im = (jnp.concatenate([column(tile, at + 64 * c), column(tile, at + 64 * c + 8)], 0) for c in range(2))
        step(pl.ds(pl.multiple_of(j * 16, 16), 16), wide(y_re), wide(y_im), 0)
        return 0

    lax.fori_loop(0, 64, begin, 0)

    gathers[0].lasts(0, 3, 1, 2)
    gathers[1].lasts(0, 3, 1, 2)

    arrive(got3, 4)
    share = got1[net.zl] + got3[...]
    for i, (p, g) in enumerate(GRANULE):
        rb[p][k * 64, g] = share[i]
    gathers[2].first()

    gathers[0].cores()
    split(net, gathers[0], amat, 0)
    gathers[2].second()
    gathers[1].cores()
    split(net, gathers[1], amat, 512)
    for d in ORDER:
        gathers[2].third(d)

    def iterate(b, frm, to):
        y_re, y_im = product(amat, pl.ds(pl.multiple_of(b * 256, 256), 256), z, frm)
        for j in range(8):
            here = slice(j * 32, j * 32 + 32)
            rows = pl.ds(pl.multiple_of(((b % 2) * 8 + j) * 64 + (b // 2) * 32, 32), 32)
            step(rows, y_re[here], y_im[here], to)

    for it in range(1, ITERS):
        frm, to = (0, 6) if it % 2 == 1 else (6, 0)

        def block(b, _, frm=frm, to=to):
            iterate(b, frm, to)
            return 0

        lax.fori_loop(0, 4, block, 0)
        if it == 1:
            gathers[2].lasts(0, 3)
        elif it == 2:
            gathers[2].lasts(1, 2)

    gathers[2].cores()
    split(net, gathers[2], rmat, 0)

    def answer(b, _):
        o_re, o_im = product(rmat, pl.ds(pl.multiple_of(b * 256, 256), 256), z, 6)
        cols = pl.ds(pl.multiple_of(b * 256, 256), 256)
        out[0, :, cols] = o_re.T
        out[1, :, cols] = o_im.T
        return 0

    lax.fori_loop(0, 2, answer, 0)

    settle(y1_part, 0)
    settle(y1_all, 1)
    settle(got1, 2)
    settle(got2, 3)
    settle(got3, 4)
    for g in gathers:
        g.end(frf_v)


def on_device(frf, mount_rows, recv_rows, codes, stiffness, loss, load):
    vmem, smem = pl.BlockSpec(memory_space=pltpu.VMEM), pl.BlockSpec(memory_space=pltpu.SMEM)
    count = codes.shape[0]
    tile = (8, 128)
    return pl.pallas_call(
        kernel,
        out_shape=jax.ShapeDtypeStruct((2, count, recv_rows.shape[0]), F32),
        in_specs=[pl.BlockSpec(memory_space=pl.ANY), smem, smem, vmem, smem, smem, vmem],
        out_specs=vmem,
        scratch_shapes=[pltpu.VMEM(frf.shape, F32)]
        + [pltpu.VMEM((128, n) + tile, F32) for n in PART * 3]
        + [
            pltpu.VMEM((6, 1024, 1024), BF16),
            pltpu.VMEM((6, 512, 1024), BF16),
            pltpu.VMEM((12, 1024, count), BF16),
            pltpu.VMEM((2, 1024, count), F32),
            pltpu.VMEM((2, 1024, 128), F32),
            pltpu.VMEM((128, 128), F32),
            pltpu.VMEM((16, 8) + tile, F32),
            pltpu.VMEM((8, 8) + tile, F32),
            pltpu.VMEM((8, 8) + tile, F32),
            pltpu.VMEM((6, 8) + tile, F32),
            pltpu.VMEM((8,) + tile, F32),
            pltpu.VMEM((1,) + tile, F32),
            pltpu.VMEM((7,) + tile, F32),
            pltpu.VMEM((1,) + tile, F32),
            pltpu.VMEM((15,) + tile, F32),
            pltpu.SemaphoreType.DMA((3,)),
            pltpu.SemaphoreType.DMA((3 * NREC,)),
            pltpu.SemaphoreType.DMA((5,)),
            pltpu.SemaphoreType.DMA((5,)),
            pltpu.SemaphoreType.DMA,
        ],
        compiler_params=pltpu.CompilerParams(collective_id=0, has_side_effects=True, vmem_limit_bytes=58 * 2**20),
        cost_estimate=pl.CostEstimate(flops=int(1.7e10), bytes_accessed=2**23, transcendentals=0),
    )(frf, mount_rows.reshape(-1), recv_rows, codes, stiffness, loss, load)


def solution(mesh):
    placed = (P(None, "row", "var"), P(), P(), P(("var", "row"), None), P(), P(), P())
    return jax.shard_map(
        on_device,
        mesh=mesh,
        in_specs=placed,
        out_specs=P(None, ("var", "row"), None),
        check_vma=False,
    )
```

profile of v0, /device:TPU:1, one launch (start us, length us, event | category | flops | bytes accessed | tf_op | source)
XLA Modules:
  0.0 93.5 jit_solution(38244040991099274)
XLA Ops:
  0.0 1.3 %copy.11.stiffness = f32[8,4]{1,0:T(8,128)} copy(f32[8,4]{0,1:T(4,128)} %param.11) | data formatting | bytes 256 | tf_op args[4]
  1.3 1.3 %copy.12.loss = f32[8,4]{1,0:T(8,128)} copy(f32[8,4]{0,1:T(4,128)} %param.12) | data formatting | bytes 256 | tf_op args[5]
  2.7 0.8 copy.10
  3.5 0.7 reshape.3.mount
  4.2 87.0 %shard_map.73 = f32[2,256,512]{2,1,0:T(8,128)} custom-call(f32[2,4096,128]{2,1,0:T(8,128)} %frf.1, s32[1024]{0:T(1024)} %reshape.3.mount, s32[512]{0:T(512)} %recv_rows.1, s32[256,256]{1,0:T(8,128)} %codes.1, f32[8,4]{1,0:T(8,128)} %copy.11.stiffness, f32[8,4]{1,0:T(8,128)} %copy.12.loss, f32[2,1024]{1,0:T(2,128)} %load.1), custom_call_target="tpu_custom_call" | custom-call | flops 16999999488 | bytes 8388608 | tf_op jit(solution)/shard_map/pallas_call | solution.py:405
  91.3 2.3 %copy.14 = f32[2,256,512]{2,1,0:T(8,128)} copy(f32[2,256,512]{2,1,0:T(8,128)} %shard_map.73) | data formatting | bytes 2097152
where the time goes:
time: 93.8 us; the launch traced here: 93.5 us
  Pallas kernels  87 us (93%)
  local copies, waits for them, and re-layouts  6.48 us (7%)
    pallas_call x1, Pallas kernels, on_device(): pl.pallas_call(kernel, out_shape=jax.ShapeDtypeStruct((2, count, recv_row...  87 us
    unnamed x4, local copies, waits for them, and re-layouts  5.76 us

commit v1 on v0

--- a/solution.py
+++ b/solution.py
@@ -140,40 +140,45 @@
     return hi, (x - hi.astype(F32)).astype(BF16)
 
 
-def put(ref, base, rows, cols, re, im):
+def put(ref, at, re, im):
     for i, x in enumerate((re, im, re + im)):
         hi, lo = halves(x)
-        ref[base + 2 * i, rows, cols] = hi
-        ref[base + 2 * i + 1, rows, cols] = lo
-
-
-def split(net, gather, mats, row_base):
-    for k in range(2):
-        axes = [[(p + q + k + gather.group) % 3 for q in range(3)] for p in range(3)]
-
-        def body(i, _, k=k, axes=axes):
-            far = (i % 4, (i // 4) % 4, i // 16)
-            at = [(net.pos[a] + far[a]) % 4 for a in range(3)]
-            row = (at[2] % 2) * 8 + at[0] * 2 + k
-            col = at[1] * 2 + at[2] // 2
-            src = [((k * 4 + far[a3]) * 4 + far[a2]) * 4 + far[a1] for a1, a2, a3 in axes]
-            cols = pl.ds(pl.multiple_of(col * 128, 128), 128)
-            tile = [gather.bufs[p][src[p], g] for p, g in GRANULE]
-            for t in range(2):
-                re = jnp.concatenate([tile[2 * t], tile[2 * t + 1]], 0)
-                im = jnp.concatenate([tile[4 + 2 * t], tile[5 + 2 * t]], 0)
-                rows = pl.ds(pl.multiple_of(row_base + row * 32 + t * 16, 16), 16)
-                put(mats, 0, rows, cols, re, im)
+        ref[at(2 * i)] = hi
+        ref[at(2 * i + 1)] = lo
+
+
+def split(net, gather, mats, row_base, cores=(0, 1)):
+    for kk in cores:
+        own = [[(p + q + kk + gather.group) % 3 for q in range(3)] for p in range(3)]
+        def add(p, a, c):
+            return ((c - net.pos[a] + 4) % 4) * 4 ** own[p].index(a)
+
+        xs = [[add(p, 0, x) + kk * 64 for x in range(4)] for p in range(3)]
+        zs = [[add(p, 2, z) for z in range(4)] for p in range(3)]
+
+        def body(y, _, kk=kk, xs=xs, zs=zs, add=add):
+            ys = [add(p, 1, y) for p in range(3)]
+            for z in range(4):
+                yz = [ys[p] + zs[p][z] for p in range(3)]
+                col = y * 2 + z // 2
+                for x in range(4):
+                    src = [yz[p] + xs[p][x] for p in range(3)]
+                    tile = [gather.bufs[p][src[p], g] for p, g in GRANULE]
+                    for t in range(2):
+                        re = jnp.concatenate([tile[2 * t], tile[2 * t + 1]], 0)
+                        im = jnp.concatenate([tile[4 + 2 * t], tile[5 + 2 * t]], 0)
+                        first = row_base + (kk * 8 + (z % 2) * 4 + x) * 32 + t * 16
+                        put(mats, lambda i: (i, col, pl.ds(first, 16)), re, im)
             return 0
 
-        lax.fori_loop(0, 64, body, 0, unroll=2)
+        lax.fori_loop(0, 4, body, 0)
 
 
 def product(mats, rows, z, base):
     dot = functools.partial(jnp.dot, preferred_element_type=F32)
     out = []
     for i in range(3):
-        a_hi, a_lo = mats[2 * i, rows, :], mats[2 * i + 1, rows, :]
+        a_hi, a_lo = (jnp.concatenate([mats[2 * i + n, c, rows, :] for c in range(8)], 1) for n in range(2))
         z_hi, z_lo = z[base + 2 * i], z[base + 2 * i + 1]
         out.append(dot(a_hi, z_hi) + (dot(a_hi, z_lo) + dot(a_lo, z_hi)))
     return out[0] - out[1], out[2] - out[0] - out[1]
@@ -185,8 +190,8 @@
 
 def kernel(frf, mount, recv_rows, codes, stiffness, loss, load, out, frf_v, *refs):
     h0, h1, rb = refs[0:3], refs[3:6], refs[6:9]
-    amat, rmat, z, delta, load_c, y1_c, picked, sum1, got1, got2, got3, y1_own, y1_part, y1_sum, y1_all = refs[9:24]
-    send, recv, misc_send, misc_recv, local = refs[24:]
+    amat, rmat, z, delta, load_c, y1_c, picked, sum1, got1, got2, got3, y1_own, y1_part, y1_sum, y1_all, found = refs[9:25]
+    send, recv, misc_send, misc_recv, local = refs[25:]
     net = Net()
     k = net.k
     whole = pltpu.make_async_copy(frf, frf_v, local)
@@ -194,9 +199,6 @@
     net.greet()
     lane = lax.broadcasted_iota(jnp.int32, (8, 128), 1)
     sub = lax.broadcasted_iota(jnp.int32, (8, 128), 0)
-
-    def column(tile, at):
-        return jnp.broadcast_to(jnp.sum(jnp.where(lane == sub + at, tile, 0.0), axis=1, keepdims=True), (8, 128))
 
     gathers = [Gather(i, bufs, send, recv, net, picked) for i, bufs in enumerate((h0, h1, rb))]
     whole.wait()
@@ -252,6 +254,12 @@
         src_ref=picked.at[other], dst_ref=got1, send_sem=misc_send.at[2], recv_sem=misc_recv.at[2],
         device_id=net.sib, device_id_type=MESH).start()
 
+    code_b = codes[...].astype(F32).astype(BF16)
+    for b in range(4):
+        mount_of = lax.broadcasted_iota(jnp.int32, (256, 256), 0) // 4 + b * 64
+        rep = (mount_of == lax.broadcasted_iota(jnp.int32, (256, 256), 1)).astype(F32).astype(BF16)
+        delta[0, pl.ds(b * 256, 256), :] = lax.dot_general(rep, code_b, (((1,), (1,)), ((), ())), preferred_element_type=F32)
+
     gathers[0].second()
     gathers[1].second()
 
@@ -275,22 +283,10 @@
     for d in ORDER:
         gathers[1].third(d)
 
-    arrive(got2, 3)
-    sums = [sum1[xx * 2 + i] + got2[i] + got2[2 + i] + got2[4 + i] for i in range(2)]
-    for i in range(2):
-        got1[i] = sums[i]
-    pltpu.make_async_remote_copy(
-        src_ref=got1.at[1 - net.zl], dst_ref=got3, send_sem=misc_send.at[4], recv_sem=misc_recv.at[4],
-        device_id=net.pair, device_id_type=MESH).start()
-
-    def load_columns(j, _):
-        rows = pl.ds(pl.multiple_of(j * 8, 8), 8)
-        c128 = pl.ds(pl.multiple_of((j // 16) * 128, 128), 128)
+    for b in range(8):
+        at = pl.ds(b * 128, 128)
         for c in range(2):
-            load_c[c, rows, :] = column(jnp.broadcast_to(load[c : c + 1, c128], (8, 128)), (j % 16) * 8)
-        return 0
-
-    lax.fori_loop(0, 128, load_columns, 0)
+            load_c[c, at, :] = jnp.broadcast_to(load[c : c + 1, at], (128, 128)).T
 
     def table(ref):
         quarter = lax.broadcasted_iota(jnp.int32, (8, 256), 0) % 4
@@ -300,11 +296,6 @@
             out.append(jnp.where(quarter == 2, ref[l, 2], jnp.where(quarter == 3, ref[l, 3], x)))
         return out
 
-    code_b = codes[...].astype(F32).astype(BF16)
-    for b in range(4):
-        mount_of = lax.broadcasted_iota(jnp.int32, (256, 256), 0) // 4 + b * 64
-        rep = (mount_of == lax.broadcasted_iota(jnp.int32, (256, 256), 1)).astype(F32).astype(BF16)
-        delta[0, pl.ds(b * 256, 256), :] = lax.dot_general(rep, code_b, (((1,), (1,)), ((), ())), preferred_element_type=F32)
     stiff_t, loss_t = table(stiffness), table(loss)
 
     def look(j, _):
@@ -318,76 +309,91 @@
         delta[1, rows, :] = s * e
         return 0
 
-    lax.fori_loop(0, 128, look, 0)
+    lax.fori_loop(0, 128, look, 0, unroll=4)
+
+    def step(rows, y_re, y_im, to):
+        d_re, d_im = delta[0, rows, :], delta[1, rows, :]
+        z_re = wide(load_c[0, rows, :]) - (d_re * y_re - d_im * y_im)
+        z_im = wide(load_c[1, rows, :]) - (d_re * y_im + d_im * y_re)
+        put(z, lambda i: (to + i, rows), z_re, z_im)
+
+    gathers[0].lasts(0)
+
+    arrive(got2, 3)
+    sums = [sum1[xx * 2 + i] + got2[i] + got2[2 + i] + got2[4 + i] for i in range(2)]
+    for i in range(2):
+        got1[i] = sums[i]
+    pltpu.make_async_remote_copy(
+        src_ref=got1.at[1 - net.zl], dst_ref=got3, send_sem=misc_send.at[4], recv_sem=misc_recv.at[4],
+        device_id=net.pair, device_id_type=MESH).start()
+
+    gathers[0].lasts(3)
 
     arrive(y1_all, 1)
     y1_c[pl.ds(net.r * 8, 8), :] = y1_sum[0]
     for i in range(15):
         y1_c[pl.ds(((net.r + 15 - i) % 16) * 8, 8), :] = y1_all[i]
 
-    def step(rows, y_re, y_im, to):
-        d_re, d_im = delta[0, rows, :], delta[1, rows, :]
-        z_re = wide(load_c[0, rows, :]) - (d_re * y_re - d_im * y_im)
-        z_im = wide(load_c[1, rows, :]) - (d_re * y_im + d_im * y_re)
-        put(z, to, rows, slice(None), z_re, z_im)
-
     def begin(j, _):
-        tile = y1_c[pl.ds(pl.multiple_of((j // 4) * 8, 8), 8), :]
-        at = (j % 4) * 16
-        y_re, y_im = (jnp.concatenate([column(tile, at + 64 * c), column(tile, at + 64 * c + 8)], 0) for c in range(2))
-        step(pl.ds(pl.multiple_of(j * 16, 16), 16), wide(y_re), wide(y_im), 0)
+        tile = y1_c[pl.ds(pl.multiple_of(j * 8, 8), 8), :]
+        both = jnp.broadcast_to(jnp.sum(tile, axis=0, keepdims=True), (128, 128)).T
+        for i in range(2):
+            step(pl.ds(pl.multiple_of(j * 64 + i * 32, 32), 32), wide(both[i * 32 : i * 32 + 32]), wide(both[64 + i * 32 : 96 + i * 32]), 0)
         return 0
 
-    lax.fori_loop(0, 64, begin, 0)
-
-    gathers[0].lasts(0, 3, 1, 2)
-    gathers[1].lasts(0, 3, 1, 2)
-
+    lax.fori_loop(0, 16, begin, 0)
+
+    gathers[0].lasts(1)
     arrive(got3, 4)
     share = got1[net.zl] + got3[...]
     for i, (p, g) in enumerate(GRANULE):
         rb[p][k * 64, g] = share[i]
     gathers[2].first()
-
+    gathers[0].lasts(2)
+
+    def iterate(first, count, frm, to):
+        y_re, y_im = product(amat, pl.ds(first, count), z, frm)
+        for j in range(count // 32):
+            here = slice(j * 32, j * 32 + 32)
+            h, i = (first // 32 + j) // 16, (first // 32 + j) % 16
+            kk, zl, x = i // 8, (i // 4) % 2, i % 4
+            rows = pl.ds((zl * 8 + x * 2 + kk) * 64 + h * 32, 32)
+            step(rows, y_re[here], y_im[here], to)
+
+    gathers[1].lasts(0)
     gathers[0].cores()
+    gathers[2].second()
     split(net, gathers[0], amat, 0)
-    gathers[2].second()
+    gathers[1].lasts(3, 1)
+    for d in ORDER:
+        gathers[2].third(d)
+    iterate(0, 512, 0, 6)
+    gathers[1].lasts(2)
     gathers[1].cores()
     split(net, gathers[1], amat, 512)
-    for d in ORDER:
-        gathers[2].third(d)
-
-    def iterate(b, frm, to):
-        y_re, y_im = product(amat, pl.ds(pl.multiple_of(b * 256, 256), 256), z, frm)
-        for j in range(8):
-            here = slice(j * 32, j * 32 + 32)
-            rows = pl.ds(pl.multiple_of(((b % 2) * 8 + j) * 64 + (b // 2) * 32, 32), 32)
-            step(rows, y_re[here], y_im[here], to)
-
-    for it in range(1, ITERS):
-        frm, to = (0, 6) if it % 2 == 1 else (6, 0)
-
-        def block(b, _, frm=frm, to=to):
-            iterate(b, frm, to)
-            return 0
-
-        lax.fori_loop(0, 4, block, 0)
-        if it == 1:
-            gathers[2].lasts(0, 3)
-        elif it == 2:
-            gathers[2].lasts(1, 2)
+    iterate(512, 512, 0, 6)
+    gathers[2].lasts(0, 3, 1, 2)
+
+    def again(it, _):
+        iterate(0, 1024, 6 - it * 6, it * 6)
+        return 0
+
+    lax.fori_loop(0, ITERS - 2, again, 0)
 
     gathers[2].cores()
     split(net, gathers[2], rmat, 0)
 
-    def answer(b, _):
-        o_re, o_im = product(rmat, pl.ds(pl.multiple_of(b * 256, 256), 256), z, 6)
-        cols = pl.ds(pl.multiple_of(b * 256, 256), 256)
-        out[0, :, cols] = o_re.T
-        out[1, :, cols] = o_im.T
+    def answer(kk, _):
+        parts = product(rmat, pl.ds(pl.multiple_of(kk * 256, 256), 256), z, 6)
+        for c in range(2):
+            for i in range(8):
+                found[c, pl.ds(pl.multiple_of(i * 64 + kk * 32, 32), 32), :] = parts[c][i * 32 : i * 32 + 32]
         return 0
 
     lax.fori_loop(0, 2, answer, 0)
+    for c in range(2):
+        for b in range(2):
+            out[c, :, pl.ds(b * 256, 256)] = found[c, pl.ds(b * 256, 256), :].T
 
     settle(y1_part, 0)
     settle(y1_all, 1)
@@ -410,8 +416,8 @@
         scratch_shapes=[pltpu.VMEM(frf.shape, F32)]
         + [pltpu.VMEM((128, n) + tile, F32) for n in PART * 3]
         + [
-            pltpu.VMEM((6, 1024, 1024), BF16),
-            pltpu.VMEM((6, 512, 1024), BF16),
+            pltpu.VMEM((6, 8, 1024, 128), BF16),
+            pltpu.VMEM((6, 8, 512, 128), BF16),
             pltpu.VMEM((12, 1024, count), BF16),
             pltpu.VMEM((2, 1024, count), F32),
             pltpu.VMEM((2, 1024, 128), F32),
@@ -425,6 +431,7 @@
             pltpu.VMEM((7,) + tile, F32),
             pltpu.VMEM((1,) + tile, F32),
             pltpu.VMEM((15,) + tile, F32),
+            pltpu.VMEM((2, 512, count), F32),
             pltpu.SemaphoreType.DMA((3,)),
             pltpu.SemaphoreType.DMA((3 * NREC,)),
             pltpu.SemaphoreType.DMA((5,)),

time: 93.8 us -> 75.8 us (0.81)
  Pallas kernels: 87 us -> 69 us
    pallas_call x1, Pallas kernels: 87 us -> 69 us  [on_device(): pl.pallas_call(kernel, out_shape=jax.ShapeDtypeStruct((2, count, recv_row...]
where the time goes in v1:
time: 75.8 us; the launch traced here: 75.5 us
  Pallas kernels  69 us (91%)
  local copies, waits for them, and re-layouts  6.48 us (9%)
    pallas_call x1, Pallas kernels, on_device(): pl.pallas_call(kernel, out_shape=jax.ShapeDtypeStruct((2, count, recv_row...  69 us
    unnamed x4, local copies, waits for them, and re-layouts  5.76 us

profile of v1, /device:TPU:1, one launch (start us, length us, event | category | flops | bytes accessed | tf_op | source)
XLA Modules:
  0.0 75.5 jit_solution(6719685349398604114)
XLA Ops:
  0.0 1.3 %copy.11.stiffness = f32[8,4]{1,0:T(8,128)} copy(f32[8,4]{0,1:T(4,128)} %param.11) | data formatting | bytes 256 | tf_op args[4]
  1.3 1.3 %copy.12.loss = f32[8,4]{1,0:T(8,128)} copy(f32[8,4]{0,1:T(4,128)} %param.12) | data formatting | bytes 256 | tf_op args[5]
  2.7 0.8 %copy.10 = s32[256,4]{1,0:T(8,128)S(1)} copy(s32[256,4]{0,1:T(4,128)} %param.8) | data formatting | bytes 8192 | tf_op args[1]
  3.5 0.7 reshape.3.mount
  4.2 69.0 %shard_map.73 = f32[2,256,512]{2,1,0:T(8,128)} custom-call(f32[2,4096,128]{2,1,0:T(8,128)} %frf.1, s32[1024]{0:T(1024)} %reshape.3.mount, s32[512]{0:T(512)} %recv_rows.1, s32[256,256]{1,0:T(8,128)} %codes.1, f32[8,4]{1,0:T(8,128)} %copy.11.stiffness, f32[8,4]{1,0:T(8,128)} %copy.12.loss, f32[2,1024]{1,0:T(2,128)} %load.1), custom_call_target="tpu_custom_call" | custom-call | flops 16999999488 | bytes 8388608 | tf_op jit(solution)/shard_map/pallas_call | solution.py:411
  73.2 2.3 %copy.14 = f32[2,256,512]{2,1,0:T(8,128)} copy(f32[2,256,512]{2,1,0:T(8,128)} %shard_map.73) | data formatting | bytes 2097152

commit v2 on v1

--- a/solution.py
+++ b/solution.py
@@ -190,8 +190,8 @@
 
 def kernel(frf, mount, recv_rows, codes, stiffness, loss, load, out, frf_v, *refs):
     h0, h1, rb = refs[0:3], refs[3:6], refs[6:9]
-    amat, rmat, z, delta, load_c, y1_c, picked, sum1, got1, got2, got3, y1_own, y1_part, y1_sum, y1_all, found = refs[9:25]
-    send, recv, misc_send, misc_recv, local = refs[25:]
+    amat, z, delta, load_c, y1_c, picked, sum1, got1, got2, got3, y1_own, y1_part, y1_sum, y1_all = refs[9:23]
+    send, recv, misc_send, misc_recv, local = refs[23:]
     net = Net()
     k = net.k
     whole = pltpu.make_async_copy(frf, frf_v, local)
@@ -209,7 +209,7 @@
     l_im = jnp.broadcast_to(load[1:2, cols], (8, 128))
     part = jnp.zeros((8, 128), F32)
     for t in range(8):
-        at = [jnp.clip(mount[net.r * 64 + t * 8 + s] - first_row, 0, 4095) for s in range(8)]
+        at = [jnp.clip(mount[s % 4, net.r * 16 + t * 2 + s // 4] - first_row, 0, 4095) for s in range(8)]
         re, im = (jnp.concatenate([frf_v[c, pl.ds(i, 1), :] for i in at], 0) for c in range(2))
         for c, x in ((0, re), (1, im)):
             p, g = GRANULE[c * 4 + t % 4]
@@ -292,8 +292,8 @@
         quarter = lax.broadcasted_iota(jnp.int32, (8, 256), 0) % 4
         out = []
         for l in range(LEVELS):
-            x = jnp.where(quarter == 0, ref[l, 0], ref[l, 1])
-            out.append(jnp.where(quarter == 2, ref[l, 2], jnp.where(quarter == 3, ref[l, 3], x)))
+            x = jnp.where(quarter == 0, ref[0, l], ref[1, l])
+            out.append(jnp.where(quarter == 2, ref[2, l], jnp.where(quarter == 3, ref[3, l], x)))
         return out
 
     stiff_t, loss_t = table(stiffness), table(loss)
@@ -319,6 +319,22 @@
 
     gathers[0].lasts(0)
 
+    gathers[0].lasts(3)
+
+    arrive(y1_all, 1)
+    y1_c[pl.ds(net.r * 8, 8), :] = y1_sum[0]
+    for i in range(15):
+        y1_c[pl.ds(((net.r + 15 - i) % 16) * 8, 8), :] = y1_all[i]
+
+    def begin(j, _):
+        tile = y1_c[pl.ds(pl.multiple_of(j * 8, 8), 8), :]
+        both = jnp.broadcast_to(jnp.sum(tile, axis=0, keepdims=True), (128, 128)).T
+        for i in range(2):
+            step(pl.ds(pl.multiple_of(j * 64 + i * 32, 32), 32), wide(both[i * 32 : i * 32 + 32]), wide(both[64 + i * 32 : 96 + i * 32]), 0)
+        return 0
+
+    lax.fori_loop(0, 16, begin, 0)
+
     arrive(got2, 3)
     sums = [sum1[xx * 2 + i] + got2[i] + got2[2 + i] + got2[4 + i] for i in range(2)]
     for i in range(2):
@@ -327,73 +343,50 @@
         src_ref=got1.at[1 - net.zl], dst_ref=got3, send_sem=misc_send.at[4], recv_sem=misc_recv.at[4],
         device_id=net.pair, device_id_type=MESH).start()
 
-    gathers[0].lasts(3)
-
-    arrive(y1_all, 1)
-    y1_c[pl.ds(net.r * 8, 8), :] = y1_sum[0]
-    for i in range(15):
-        y1_c[pl.ds(((net.r + 15 - i) % 16) * 8, 8), :] = y1_all[i]
-
-    def begin(j, _):
-        tile = y1_c[pl.ds(pl.multiple_of(j * 8, 8), 8), :]
-        both = jnp.broadcast_to(jnp.sum(tile, axis=0, keepdims=True), (128, 128)).T
-        for i in range(2):
-            step(pl.ds(pl.multiple_of(j * 64 + i * 32, 32), 32), wide(both[i * 32 : i * 32 + 32]), wide(both[64 + i * 32 : 96 + i * 32]), 0)
-        return 0
-
-    lax.fori_loop(0, 16, begin, 0)
-
-    gathers[0].lasts(1)
+    gathers[0].lasts(1, 2)
+
+    gathers[1].lasts(0)
     arrive(got3, 4)
     share = got1[net.zl] + got3[...]
     for i, (p, g) in enumerate(GRANULE):
         rb[p][k * 64, g] = share[i]
     gathers[2].first()
-    gathers[0].lasts(2)
-
-    def iterate(first, count, frm, to):
-        y_re, y_im = product(amat, pl.ds(first, count), z, frm)
-        for j in range(count // 32):
-            here = slice(j * 32, j * 32 + 32)
-            h, i = (first // 32 + j) // 16, (first // 32 + j) % 16
-            kk, zl, x = i // 8, (i // 4) % 2, i % 4
-            rows = pl.ds((zl * 8 + x * 2 + kk) * 64 + h * 32, 32)
-            step(rows, y_re[here], y_im[here], to)
-
-    gathers[1].lasts(0)
     gathers[0].cores()
-    gathers[2].second()
     split(net, gathers[0], amat, 0)
     gathers[1].lasts(3, 1)
-    for d in ORDER:
-        gathers[2].third(d)
-    iterate(0, 512, 0, 6)
-    gathers[1].lasts(2)
-    gathers[1].cores()
-    split(net, gathers[1], amat, 512)
-    iterate(512, 512, 0, 6)
-    gathers[2].lasts(0, 3, 1, 2)
-
-    def again(it, _):
-        iterate(0, 1024, 6 - it * 6, it * 6)
+
+    def unit(u, _):
+        @pl.when(u == 1)
+        def _():
+            gathers[1].lasts(2)
+            gathers[2].second()
+            gathers[1].cores()
+            split(net, gathers[1], amat, 512)
+            for d in ORDER:
+                gathers[2].third(d)
+
+        @pl.when(u == 4)
+        def _():
+            gathers[2].lasts(0, 3, 1, 2)
+
+        @pl.when(u == 2 * ITERS - 2)
+        def _():
+            gathers[2].cores()
+            split(net, gathers[2], amat, 1024)
+
+        h, frm = u % 2, ((u // 2) % 2) * 6
+        first = jnp.where(u == 2 * ITERS - 2, 1024, h * 512)
+        y_re, y_im = product(amat, pl.ds(pl.multiple_of(first, 512), 512), z, frm)
+        for j in range(16):
+            here = slice(j * 32, j * 32 + 32)
+            kk, zl, x = j // 8, (j // 4) % 2, j % 4
+            to = (zl * 8 + x * 2 + kk) * 32
+            out[0, pl.ds(to, 32), :] = y_re[here]
+            out[1, pl.ds(to, 32), :] = y_im[here]
+            step(pl.ds(pl.multiple_of(to * 2 + h * 32, 32), 32), y_re[here], y_im[here], 6 - frm)
         return 0
 
-    lax.fori_loop(0, ITERS - 2, again, 0)
-
-    gathers[2].cores()
-    split(net, gathers[2], rmat, 0)
-
-    def answer(kk, _):
-        parts = product(rmat, pl.ds(pl.multiple_of(kk * 256, 256), 256), z, 6)
-        for c in range(2):
-            for i in range(8):
-                found[c, pl.ds(pl.multiple_of(i * 64 + kk * 32, 32), 32), :] = parts[c][i * 32 : i * 32 + 32]
-        return 0
-
-    lax.fori_loop(0, 2, answer, 0)
-    for c in range(2):
-        for b in range(2):
-            out[c, :, pl.ds(b * 256, 256)] = found[c, pl.ds(b * 256, 256), :].T
+    lax.fori_loop(0, 2 * ITERS - 1, unit, 0)
 
     settle(y1_part, 0)
     settle(y1_all, 1)
@@ -408,16 +401,15 @@
     vmem, smem = pl.BlockSpec(memory_space=pltpu.VMEM), pl.BlockSpec(memory_space=pltpu.SMEM)
     count = codes.shape[0]
     tile = (8, 128)
-    return pl.pallas_call(
+    found = pl.pallas_call(
         kernel,
-        out_shape=jax.ShapeDtypeStruct((2, count, recv_rows.shape[0]), F32),
+        out_shape=jax.ShapeDtypeStruct((2, recv_rows.shape[0], count), F32),
         in_specs=[pl.BlockSpec(memory_space=pl.ANY), smem, smem, vmem, smem, smem, vmem],
         out_specs=vmem,
         scratch_shapes=[pltpu.VMEM(frf.shape, F32)]
         + [pltpu.VMEM((128, n) + tile, F32) for n in PART * 3]
         + [
-            pltpu.VMEM((6, 8, 1024, 128), BF16),
-            pltpu.VMEM((6, 8, 512, 128), BF16),
+            pltpu.VMEM((6, 8, 1536, 128), BF16),
             pltpu.VMEM((12, 1024, count), BF16),
             pltpu.VMEM((2, 1024, count), F32),
             pltpu.VMEM((2, 1024, 128), F32),
@@ -431,7 +423,6 @@
             pltpu.VMEM((7,) + tile, F32),
             pltpu.VMEM((1,) + tile, F32),
             pltpu.VMEM((15,) + tile, F32),
-            pltpu.VMEM((2, 512, count), F32),
             pltpu.SemaphoreType.DMA((3,)),
             pltpu.SemaphoreType.DMA((3 * NREC,)),
             pltpu.SemaphoreType.DMA((5,)),
@@ -440,7 +431,8 @@
         ],
         compiler_params=pltpu.CompilerParams(collective_id=0, has_side_effects=True, vmem_limit_bytes=58 * 2**20),
         cost_estimate=pl.CostEstimate(flops=int(1.7e10), bytes_accessed=2**23, transcendentals=0),
-    )(frf, mount_rows.reshape(-1), recv_rows, codes, stiffness, loss, load)
+    )(frf, mount_rows.T, recv_rows, codes, stiffness.T, loss.T, load)
+    return jnp.swapaxes(found, 1, 2)
 
 
 def solution(mesh):

time: 75.8 us -> 65.2 us (0.86)
  Pallas kernels: 69 us -> 61.9 us
  local copies, waits for them, and re-layouts: 6.48 us -> 2.53 us
    pallas_call x1, Pallas kernels: 69 us -> 61.9 us  [on_device(): pl.pallas_call(kernel, out_shape=jax.ShapeDtypeStruct((2, recv_rows.shape...]
    unnamed x4 -> x0, local copies, waits for them, and re-layouts: 5.76 us -> none
    transpose x0 -> x1, local copies, waits for them, and re-layouts: none -> 2.53 us  [on_device(): return jnp.swapaxes(found, 1, 2)]
where the time goes in v2:
time: 65.2 us; the launch traced here: 64.4 us
  Pallas kernels  61.9 us (95%)
  local copies, waits for them, and re-layouts  2.53 us (4%)
    pallas_call x1, Pallas kernels, on_device(): pl.pallas_call(kernel, out_shape=jax.ShapeDtypeStruct((2, recv_rows.shape...  61.9 us
    transpose x1, local copies, waits for them, and re-layouts, on_device(): return jnp.swapaxes(found, 1, 2)  2.53 us

profile of v2, /device:TPU:1, one launch (start us, length us, event | category | flops | bytes accessed | tf_op | source)
XLA Modules:
  0.0 64.4 jit_solution(773886959589738846)
XLA Ops:
  0.0 61.9 %shard_map.73 = f32[2,512,256]{2,1,0:T(8,128)} custom-call(f32[2,4096,128]{2,1,0:T(8,128)} %frf.1, s32[4,256]{1,0:T(4,128)} %bitcast.5, s32[512]{0:T(512)} %recv_rows.1, s32[256,256]{1,0:T(8,128)} %codes.1, f32[4,8]{1,0:T(4,128)} %bitcast.6, f32[4,8]{1,0:T(4,128)} %bitcast.7, f32[2,1024]{1,0:T(2,128)} %load.1), custom_call_target="tpu_custom_call" | custom-call | flops 16999999488 | bytes 8388608 | tf_op jit(solution)/shard_map/pallas_call | solution.py:404
  61.9 2.5 %copy.8 = f32[2,256,512]{2,1,0:T(8,128)} copy(f32[2,256,512]{1,2,0:T(8,128)} %bitcast.4) | data formatting | bytes 2097152 | tf_op jit(solution)/shard_map/transpose | solution.py:435

commit v3 on v2

--- a/solution.py
+++ b/solution.py
@@ -362,12 +362,19 @@
             gathers[2].second()
             gathers[1].cores()
             split(net, gathers[1], amat, 512)
+
+        @pl.when(u == 2)
+        def _():
             for d in ORDER:
                 gathers[2].third(d)
 
         @pl.when(u == 4)
         def _():
-            gathers[2].lasts(0, 3, 1, 2)
+            gathers[2].lasts(0, 3)
+
+        @pl.when(u == 5)
+        def _():
+            gathers[2].lasts(1, 2)
 
         @pl.when(u == 2 * ITERS - 2)
         def _():

time: 65.2 us -> 64.4 us (0.988)
  no operation moved by 1% of the time
where the time goes in v3:
time: 64.4 us; the launch traced here: 64.2 us
  Pallas kernels  61.7 us (96%)
  local copies, waits for them, and re-layouts  2.53 us (4%)
    pallas_call x1, Pallas kernels, on_device(): pl.pallas_call(kernel, out_shape=jax.ShapeDtypeStruct((2, recv_rows.shape...  61.7 us
    transpose x1, local copies, waits for them, and re-layouts, on_device(): return jnp.swapaxes(found, 1, 2)  2.53 us

profile of v3, /device:TPU:1, one launch (start us, length us, event | category | flops | bytes accessed | tf_op | source)
XLA Modules:
  0.0 64.2 jit_solution(1754310767079191788)
XLA Ops:
  0.0 61.7 %shard_map.73 = f32[2,512,256]{2,1,0:T(8,128)} custom-call(f32[2,4096,128]{2,1,0:T(8,128)} %frf.1, s32[4,256]{1,0:T(4,128)} %bitcast.5, s32[512]{0:T(512)} %recv_rows.1, s32[256,256]{1,0:T(8,128)} %codes.1, f32[4,8]{1,0:T(4,128)} %bitcast.6, f32[4,8]{1,0:T(4,128)} %bitcast.7, f32[2,1024]{1,0:T(2,128)} %load.1), custom_call_target="tpu_custom_call" | custom-call | flops 16999999488 | bytes 8388608 | tf_op jit(solution)/shard_map/pallas_call | solution.py:411
  61.7 2.5 %copy.8 = f32[2,256,512]{2,1,0:T(8,128)} copy(f32[2,256,512]{1,2,0:T(8,128)} %bitcast.4) | data formatting | bytes 2097152 | tf_op jit(solution)/shard_map/transpose | solution.py:442

commit v4 on v3

--- a/solution.py
+++ b/solution.py
@@ -107,6 +107,8 @@
         self.wait(3, self.sem("a"))
         for p in range(3):
             self.send_b(p, (1, 3))
+
+    def second_c(self):
         for p in range(3):
             self.send_c(p, 0, (1, 3))
         self.core(0, 0)
@@ -262,6 +264,8 @@
 
     gathers[0].second()
     gathers[1].second()
+    gathers[0].second_c()
+    gathers[1].second_c()
 
     arrive(y1_part, 0)
     total = y1_own[0]
@@ -319,8 +323,6 @@
 
     gathers[0].lasts(0)
 
-    gathers[0].lasts(3)
-
     arrive(y1_all, 1)
     y1_c[pl.ds(net.r * 8, 8), :] = y1_sum[0]
     for i in range(15):
@@ -333,7 +335,7 @@
             step(pl.ds(pl.multiple_of(j * 64 + i * 32, 32), 32), wide(both[i * 32 : i * 32 + 32]), wide(both[64 + i * 32 : 96 + i * 32]), 0)
         return 0
 
-    lax.fori_loop(0, 16, begin, 0)
+    lax.fori_loop(0, 16, begin, 0, unroll=2)
 
     arrive(got2, 3)
     sums = [sum1[xx * 2 + i] + got2[i] + got2[2 + i] + got2[4 + i] for i in range(2)]
@@ -343,6 +345,7 @@
         src_ref=got1.at[1 - net.zl], dst_ref=got3, send_sem=misc_send.at[4], recv_sem=misc_recv.at[4],
         device_id=net.pair, device_id_type=MESH).start()
 
+    gathers[0].lasts(3)
     gathers[0].lasts(1, 2)
 
     gathers[1].lasts(0)
@@ -360,6 +363,7 @@
         def _():
             gathers[1].lasts(2)
             gathers[2].second()
+            gathers[2].second_c()
             gathers[1].cores()
             split(net, gathers[1], amat, 512)
 

time: 64.4 us -> 64.4 us (level)
  no operation moved by 1% of the time
where the time goes in v4:
time: 64.4 us; the launch traced here: 64.2 us
  Pallas kernels  61.7 us (96%)
  local copies, waits for them, and re-layouts  2.53 us (4%)
    pallas_call x1, Pallas kernels, on_device(): pl.pallas_call(kernel, out_shape=jax.ShapeDtypeStruct((2, recv_rows.shape...  61.7 us
    transpose x1, local copies, waits for them, and re-layouts, on_device(): return jnp.swapaxes(found, 1, 2)  2.53 us

profile of v4, /device:TPU:1, one launch (start us, length us, event | category | flops | bytes accessed | tf_op | source)
XLA Modules:
  0.0 64.2 jit_solution(12004764717238179065)
XLA Ops:
  0.0 61.7 %shard_map.73 = f32[2,512,256]{2,1,0:T(8,128)} custom-call(f32[2,4096,128]{2,1,0:T(8,128)} %frf.1, s32[4,256]{1,0:T(4,128)} %bitcast.5, s32[512]{0:T(512)} %recv_rows.1, s32[256,256]{1,0:T(8,128)} %codes.1, f32[4,8]{1,0:T(4,128)} %bitcast.6, f32[4,8]{1,0:T(4,128)} %bitcast.7, f32[2,1024]{1,0:T(2,128)} %load.1), custom_call_target="tpu_custom_call" | custom-call | flops 16999999488 | bytes 8388608 | tf_op jit(solution)/shard_map/pallas_call | solution.py:415
  61.7 2.5 %copy.8 = f32[2,256,512]{2,1,0:T(8,128)} copy(f32[2,256,512]{1,2,0:T(8,128)} %bitcast.4) | data formatting | bytes 2097152 | tf_op jit(solution)/shard_map/transpose | solution.py:446
